TPU v7x, 32 devices: a whole 2x2x4 slice. The times are simulated.
32 devices in a mesh: gx: 8 (over y, x, core), gy: 4 (over z).
Axes of the slice: x: 2, y: 2, z: 4, core: 2. Of those that a mesh axis runs over, the one named last changes fastest.
Arguments:
- u_now: float32 [3, 6, 64, 512], P(None, None, 'gx', 'gy'), may hold values from -6 to 6
- u_prev: float32 [3, 6, 64, 512], P(None, None, 'gx', 'gy'), may hold values from -6 to 6
- lame_lambda: float32 [6, 64, 512], P(None, 'gx', 'gy'), may hold values from 0.5 to 1.5
- lame_mu: float32 [6, 64, 512], P(None, 'gx', 'gy'), may hold values from 0.3 to 1
- buoyancy: float32 [6, 64, 512], P(None, 'gx', 'gy'), may hold values from 0.5 to 1
- q_now: float32 [2048, 128], P(('gx', 'gy')), may hold values from -3 to 3
- q_prev: float32 [2048, 128], P(('gx', 'gy')), may hold values from -3 to 3
- archetype: int32 [2048], P(('gx', 'gy')), may hold values from 0 to 7
- stiffness: float32 [8, 128, 128], replicated, may hold values from -1.2 to 14, as said below
- couple: float32 [8, 3, 128], replicated, may hold values from -1.5 to 1.5
- counts: int32 [8, 4, 4], P('gx'), may hold values from 1 to 16, as said below
- footprint: int32 [8, 4, 256], P('gx', 'gy'), may hold values from 0 to 1023, as said below
Outputs:
- u_last: float32 [3, 6, 64, 512], P(None, None, 'gx', 'gy')
- u_before: float32 [3, 6, 64, 512], P(None, None, 'gx', 'gy')
- q_last: float32 [2048, 128], P(('gx', 'gy'))
- q_before: float32 [2048, 128], P(('gx', 'gy'))
Inputs may be any that keep to these rules, and one draw needn't show every extreme that they name: `stiffness`: symmetric, one matrix for each archetype. `counts`: at most 16; in every tile row some owner column receives 16 from every home column. `footprint`: the 4 cells of a slot form a 2 x 2 square of the home tile's surface, numbered x * 128 + y.
All inputs are finite; a program needn't handle non-finite values.
Results may differ from a plain program's by a relative error of at most 0.0001.
Values sent between devices are 32-bit elements; how exact they have to be, the bound alone decides.
A program may use at most 64 MiB of HBM per device.

v0:
```python
import jax
import jax.numpy as jnp
from jax import lax
from jax.sharding import PartitionSpec as P

FRAME_FREEDOMS = 128
FOOTPRINT_CELLS = 4
STEPS = 2
time_step = 0.25


def with_halo(array, sides, width):
    for axis, dim in sides:
        devices, length = (lax.axis_size(axis), array.shape[dim])
        up = [(i, (i + 1) % devices) for i in range(devices - 1)]
        down = [(j, i) for i, j in up]
        last = lax.slice_in_dim(array, length - width, length, axis=dim)
        initial = lax.slice_in_dim(array, 0, width, axis=dim)
        before = lax.ppermute(last, axis, up)
        after = lax.ppermute(initial, axis, down)
        array = jnp.concatenate([before, array, after], axis=dim)
    return array


def derive(padded, along):
    field = padded
    for other in (1, 2, 3):
        if other != along:
            field = lax.slice_in_dim(field, 2, field.shape[other] - 2, axis=other)
    length = field.shape[along] - 4

    def window(offset):
        return lax.slice_in_dim(field, offset, offset + length, axis=along)

    return (8.0 * (window(3) - window(1)) - (window(4) - window(0))) / 12.0


def stress_of(padded, lam_field, mu_field):
    grad_x = derive(padded, 2)
    grad_y = derive(padded, 3)
    grad_z = derive(padded, 1)
    trace = grad_x[0] + grad_y[1] + grad_z[2]
    return jnp.stack(
        [
            lam_field * trace + 2.0 * mu_field * grad_x[0],
            lam_field * trace + 2.0 * mu_field * grad_y[1],
            lam_field * trace + 2.0 * mu_field * grad_z[2],
            mu_field * (grad_y[0] + grad_x[1]),
            mu_field * (grad_z[0] + grad_x[2]),
            mu_field * (grad_z[1] + grad_y[2]),
        ]
    )


def divergence(padded):
    grad_x = derive(padded, 2)
    grad_y = derive(padded, 3)
    grad_z = derive(padded, 1)
    return jnp.stack(
        [
            grad_x[0] + grad_y[3] + grad_z[4],
            grad_x[3] + grad_y[1] + grad_z[5],
            grad_x[4] + grad_y[5] + grad_z[2],
        ]
    )


def pad_depth(field):
    return jnp.pad(field, ((0, 0), (2, 2), (0, 0), (0, 0)))


def shards(
    u_now,
    u_prev,
    lame_lambda,
    lame_mu,
    buoyancy,
    q_now,
    q_prev,
    archetype,
    stiffness,
    couple,
    counts,
    footprint,
):
    highest = lax.Precision.HIGHEST
    cells_x = u_now.shape[2]
    cells_y = u_now.shape[3]
    owners = lax.axis_size("gy")
    slots = q_now.shape[0]
    capacity = slots // owners
    home = lax.axis_index("gy")
    cells = footprint[0, 0]
    row_counts = lax.dynamic_index_in_dim(counts[0], home, 0, keepdims=False)
    active_slots = (
        (jnp.arange(capacity, dtype=jnp.int32)[None, :] < row_counts[:, None])
        .astype(jnp.float32)
        .reshape(slots)
    )
    kinds = stiffness.shape[0]
    onehot = (archetype[:, None] == jnp.arange(kinds, dtype=jnp.int32)[None, :]).astype(jnp.float32)
    stiff_table = stiffness.transpose(2, 0, 1).reshape(FRAME_FREEDOMS, kinds * FRAME_FREEDOMS)
    drive_table = couple.transpose(1, 0, 2).reshape(3, kinds * FRAME_FREEDOMS)
    shear_table = couple.transpose(2, 0, 1).reshape(FRAME_FREEDOMS, kinds * 3)
    field, older = (u_now, u_prev)
    frame_state, prior_frame_state = (q_now, q_prev)
    for counter in range(STEPS):
        surface = field[:, 0].reshape(3, cells_x * cells_y)
        base_layer = (
            surface[:, cells].reshape(3, slots, FOOTPRINT_CELLS).sum(axis=2)
            / FOOTPRINT_CELLS
            * active_slots
        )
        ground_motion = lax.all_to_all(base_layer, "gy", split_axis=1, concat_axis=1, tiled=True)
        shear_all = jnp.dot(frame_state, shear_table, precision=highest).reshape(slots, kinds, 3)
        shear_force = jnp.sum(shear_all * onehot[:, :, None], axis=1)
        returned = (
            lax.all_to_all(shear_force.T, "gy", split_axis=1, concat_axis=1, tiled=True)
            * active_slots
        )
        contrib = jnp.repeat(returned / FOOTPRINT_CELLS, FOOTPRINT_CELLS, axis=1)
        force = (
            jnp.zeros((3, cells_x * cells_y), jnp.float32)
            .at[:, cells]
            .add(contrib)
            .reshape(3, cells_x, cells_y)
        )
        rimmed = with_halo(field, (("gx", 2), ("gy", 3)), 2)
        inner = stress_of(pad_depth(rimmed), lame_lambda, lame_mu)
        stress = with_halo(inner, (("gx", 2), ("gy", 3)), 2)
        total = divergence(pad_depth(stress))
        total = total.at[:, 0].add(force)
        field_new = 2.0 * field - older + time_step * time_step * (buoyancy * total)
        stiff_all = jnp.dot(frame_state, stiff_table, precision=highest).reshape(
            slots, kinds, FRAME_FREEDOMS
        )
        stiff_term = jnp.sum(stiff_all * onehot[:, :, None], axis=1)
        drive_all = jnp.dot(ground_motion.T, drive_table, precision=highest).reshape(
            slots, kinds, FRAME_FREEDOMS
        )
        drive = jnp.sum(drive_all * onehot[:, :, None], axis=1)
        next_frame_state = (
            2.0 * frame_state - prior_frame_state + time_step * time_step * (drive - stiff_term)
        )
        older, field = (field, field_new)
        prior_frame_state, frame_state = (frame_state, next_frame_state)
    return (field, older, frame_state, prior_frame_state)


def solution(mesh):
    return jax.shard_map(
        shards,
        mesh=mesh,
        in_specs=(
            P(None, None, "gx", "gy"),
            P(None, None, "gx", "gy"),
            P(None, "gx", "gy"),
            P(None, "gx", "gy"),
            P(None, "gx", "gy"),
            P(("gx", "gy"), None),
            P(("gx", "gy"), None),
            P(("gx", "gy")),
            P(),
            P(),
            P("gx", None, None),
            P("gx", "gy", None),
        ),
        out_specs=(
            P(None, None, "gx", "gy"),
            P(None, None, "gx", "gy"),
            P(("gx", "gy"), None),
            P(("gx", "gy"), None),
        ),
        check_vma=False,
    )
```

profile of v0, /device:TPU:18, one launch (start us, length us, event | category | flops | bytes accessed | tf_op | source)
XLA Modules:
  0.0 116.6 jit_solution(14297653245160464524)
XLA Ops:
  0.7 1.0 fusion.106
  1.7 1.9 %collective-permute-start.1 = (f32[3,6,2,128]{3,2,1,0:T(2,128)S(1)}, f32[3,6,2,128]{3,2,1,0:T(2,128)S(1)}, u32[]{:S(2)}, u32[]{:S(2)}) collective-permute-start(f32[3,6,2,128]{3,2,1,0:T(2,128)S(1)} %get-tuple-element.55), channel_id=1, source_target_pairs={{0,4},{4,8},{8,12},{12,16},{16,20},{20,24},{24,28},{1,5},{5,9},{9,... | collective-permute-start | bytes 55304 | tf_op jit(solution)/shard_map/ppermute | solution.py:19
  3.6 3.6 %collective-permute-start = (f32[3,6,2,128]{3,2,1,0:T(2,128)S(1)}, f32[3,6,2,128]{3,2,1,0:T(2,128)S(1)}, u32[]{:S(2)}, u32[]{:S(2)}) collective-permute-start(f32[3,6,2,128]{3,2,1,0:T(2,128)S(1)} %get-tuple-element.54), channel_id=1, source_target_pairs={{4,0},{8,4},{12,8},{16,12},{20,16},{24,20},{28,24},{5,1},{9,5},{13... | collective-permute-start | bytes 55304 | tf_op jit(solution)/shard_map/ppermute | solution.py:20
  7.3 0.6 copy-done.12
  8.3 0.6 copy.42
  8.9 5.2 %all-to-all-start = ((f32[3,4,16]{2,0,1:T(4,128)}), f32[3,4,16]{2,0,1:T(4,128)S(1)}, u32[]{:S(2)}, u32[]{:S(2)}) async-start(f32[3,4,16]{2,0,1:T(4,128)} %copy.42), calls=%async_computation | async-start | bytes 16384 | tf_op jit(solution)/shard_map/all_to_all | solution.py:118
  14.1 0.7 fusion.98
  14.9 0.6 copy-done.11
  15.6 0.7 fusion.2
  16.6 3.4 %collective-permute-start.3 = (f32[3,6,12,2]{3,2,1,0:T(8,128)S(1)}, f32[3,6,12,2]{3,2,1,0:T(8,128)S(1)}, u32[]{:S(2)}, u32[]{:S(2)}) collective-permute-start(f32[3,6,12,2]{3,2,1,0:T(8,128)S(1)} %get-tuple-element.48), channel_id=1, source_target_pairs={{0,1},{1,2},{2,3},{4,5},{5,6},{6,7},{8,9},{9,10},{10,11},{12,13},{... | collective-permute-start | bytes 5192 | tf_op jit(solution)/shard_map/ppermute | solution.py:19
  20.0 2.5 %collective-permute-start.2 = (f32[3,6,12,2]{3,2,1,0:T(8,128)S(1)}, f32[3,6,12,2]{3,2,1,0:T(8,128)S(1)}, u32[]{:S(2)}, u32[]{:S(2)}) collective-permute-start(f32[3,6,12,2]{3,2,1,0:T(8,128)S(1)} %get-tuple-element.49), channel_id=1, source_target_pairs={{1,0},{2,1},{3,2},{5,4},{6,5},{7,6},{9,8},{10,9},{11,10},{13,12},{... | collective-permute-start | bytes 5192 | tf_op jit(solution)/shard_map/ppermute | solution.py:20
  22.5 0.6 slice-done
  23.2 0.2 copy.46
  23.4 0.7 gather_fusion
  24.4 2.6 %collective-permute-done.2 = f32[3,6,12,2]{3,2,1,0:T(8,128)S(1)} collective-permute-done((f32[3,6,12,2]{3,2,1,0:T(8,128)S(1)}, f32[3,6,12,2]{3,2,1,0:T(8,128)S(1)}, u32[]{:S(2)}, u32[]{:S(2)}) %collective-permute-start.2) | collective-permute-done | bytes 1760 | tf_op jit(solution)/shard_map/ppermute | solution.py:20
  27.0 0.3 fusion.64
  27.3 0.3 select_maximum_fusion.12
  27.7 0.6 copy-done.1
  28.5 1.9 %collective-permute-start.4 = (f32[6,6,2,128]{3,2,1,0:T(2,128)S(1)}, f32[6,6,2,128]{3,2,1,0:T(2,128)S(1)}, u32[]{:S(2)}, u32[]{:S(2)}) collective-permute-start(f32[6,6,2,128]{3,2,1,0:T(2,128)S(1)} %get-tuple-element.47), channel_id=1, source_target_pairs={{4,0},{8,4},{12,8},{16,12},{20,16},{24,20},{28,24},{5,1},{9,5},{13... | collective-permute-start | bytes 110600 | tf_op jit(solution)/shard_map/ppermute | solution.py:20
  30.4 2.4 %collective-permute-start.5 = (f32[6,6,2,128]{3,2,1,0:T(2,128)S(1)}, f32[6,6,2,128]{3,2,1,0:T(2,128)S(1)}, u32[]{:S(2)}, u32[]{:S(2)}) collective-permute-start(f32[6,6,2,128]{3,2,1,0:T(2,128)S(1)} %get-tuple-element.46), channel_id=1, source_target_pairs={{0,4},{4,8},{8,12},{12,16},{16,20},{20,24},{24,28},{1,5},{5,9},{9,... | collective-permute-start | bytes 110600 | tf_op jit(solution)/shard_map/ppermute | solution.py:19
  32.9 1.6 %scatter_custom_fusion = f32[3,1024]{0,1:T(8,128)S(1)} fusion(s32[256]{0:T(256)S(1)} %bitcast.205, f32[256,3]{1,0:T(8,128)S(1)} %bitcast.197, f32[]{:T(128)} %constant.90.clone.1), kind=kCustom, calls=%fused_computation.50 | custom fusion | flops 768 | bytes 12292 | tf_op jit(solution)/shard_map/scatter-add | solution.py:125
  34.7 1.0 collective-permute-done.5
  35.9 2.5 %collective-permute-start.6 = (f32[6,6,12,2]{3,2,1,0:T(8,128)S(1)}, f32[6,6,12,2]{3,2,1,0:T(8,128)S(1)}, u32[]{:S(2)}, u32[]{:S(2)}) collective-permute-start(f32[6,6,12,2]{3,2,1,0:T(8,128)S(1)} %get-tuple-element.41), channel_id=1, source_target_pairs={{1,0},{2,1},{3,2},{5,4},{6,5},{7,6},{9,8},{10,9},{11,10},{13,12},{... | collective-permute-start | bytes 10376 | tf_op jit(solution)/shard_map/ppermute | solution.py:20
  38.3 3.4 %collective-permute-start.7 = (f32[6,6,12,2]{3,2,1,0:T(8,128)S(1)}, f32[6,6,12,2]{3,2,1,0:T(8,128)S(1)}, u32[]{:S(2)}, u32[]{:S(2)}) collective-permute-start(f32[6,6,12,2]{3,2,1,0:T(8,128)S(1)} %get-tuple-element.40), channel_id=1, source_target_pairs={{0,1},{1,2},{2,3},{4,5},{5,6},{6,7},{8,9},{9,10},{10,11},{12,13},{... | collective-permute-start | bytes 10376 | tf_op jit(solution)/shard_map/ppermute | solution.py:19
  41.9 5.7 %collective-permute-done.6 = f32[6,6,12,2]{3,2,1,0:T(8,128)S(1)} collective-permute-done((f32[6,6,12,2]{3,2,1,0:T(8,128)S(1)}, f32[6,6,12,2]{3,2,1,0:T(8,128)S(1)}, u32[]{:S(2)}, u32[]{:S(2)}) %collective-permute-start.6) | collective-permute-done | bytes 3488 | tf_op jit(solution)/shard_map/ppermute | solution.py:20
  47.6 2.3 %collective-permute-done.7 = f32[6,6,12,2]{3,2,1,0:T(8,128)S(1)} collective-permute-done((f32[6,6,12,2]{3,2,1,0:T(8,128)S(1)}, f32[6,6,12,2]{3,2,1,0:T(8,128)S(1)}, u32[]{:S(2)}, u32[]{:S(2)}) %collective-permute-start.7) | collective-permute-done | bytes 3488 | tf_op jit(solution)/shard_map/ppermute | solution.py:19
  49.9 0.5 select_maximum_fusion.4
  50.4 0.2 fusion.33
  50.6 0.5 fusion.37
  51.2 0.8 copy-done.8
  52.1 0.2 copy.54
  52.3 0.7 gather_fusion.1
  53.2 0.6 broadcast_multiply_fusion
  53.8 5.1 %all-to-all-start.1 = ((f32[3,4,16]{2,0,1:T(4,128)}), f32[3,4,16]{2,0,1:T(4,128)S(1)}, u32[]{:S(2)}, u32[]{:S(2)}) async-start(f32[3,4,16]{2,0,1:T(4,128)} %get-tuple-element.57), calls=%async_computation.1 | async-start | bytes 16384 | tf_op jit(solution)/shard_map/all_to_all | solution.py:114
  58.9 1.9 %collective-permute-start.9 = (f32[3,6,2,128]{3,2,1,0:T(2,128)S(1)}, f32[3,6,2,128]{3,2,1,0:T(2,128)S(1)}, u32[]{:S(2)}, u32[]{:S(2)}) collective-permute-start(f32[3,6,2,128]{3,2,1,0:T(2,128)S(1)} %get-tuple-element.51), channel_id=1, source_target_pairs={{0,4},{4,8},{8,12},{12,16},{16,20},{20,24},{24,28},{1,5},{5,9},{9,... | collective-permute-start | bytes 55304 | tf_op jit(solution)/shard_map/ppermute | solution.py:19
  60.9 3.6 %collective-permute-start.8 = (f32[3,6,2,128]{3,2,1,0:T(2,128)S(1)}, f32[3,6,2,128]{3,2,1,0:T(2,128)S(1)}, u32[]{:S(2)}, u32[]{:S(2)}) collective-permute-start(f32[3,6,2,128]{3,2,1,0:T(2,128)S(1)} %get-tuple-element.50), channel_id=1, source_target_pairs={{4,0},{8,4},{12,8},{16,12},{20,16},{24,20},{28,24},{5,1},{9,5},{13... | collective-permute-start | bytes 55304 | tf_op jit(solution)/shard_map/ppermute | solution.py:20
  64.5 5.1 %all-to-all-start.3 = ((f32[3,4,16]{2,0,1:T(4,128)}), f32[3,4,16]{2,0,1:T(4,128)S(1)}, u32[]{:S(2)}, u32[]{:S(2)}) async-start(f32[3,4,16]{2,0,1:T(4,128)} %get-tuple-element.56), calls=%async_computation.3 | async-start | bytes 16384 | tf_op jit(solution)/shard_map/all_to_all | solution.py:114
  69.7 0.4 fusion
  70.2 0.3 copy-done.9
  70.5 0.7 fusion.3
  71.5 0.6 copy.50
  72.1 0.8 all-to-all-done.3
  72.9 5.6 %all-to-all-start.2 = ((f32[3,4,16]{2,0,1:T(4,128)}), f32[3,4,16]{2,0,1:T(4,128)S(1)}, u32[]{:S(2)}, u32[]{:S(2)}) async-start(f32[3,4,16]{2,0,1:T(4,128)} %copy.50), calls=%async_computation.2 | async-start | bytes 16384 | tf_op jit(solution)/shard_map/all_to_all | solution.py:118
  78.5 0.4 fusion.1
  79.0 0.6 multiply_add_fusion.2
  79.6 2.1 %all-to-all-done.2 = f32[3,4,16]{2,0,1:T(4,128)S(1)} async-done(((f32[3,4,16]{2,0,1:T(4,128)}), f32[3,4,16]{2,0,1:T(4,128)S(1)}, u32[]{:S(2)}, u32[]{:S(2)}) %all-to-all-start.2) | async-done | bytes 800 | tf_op jit(solution)/shard_map/all_to_all | solution.py:118
  81.9 3.4 %collective-permute-start.10 = (f32[3,6,12,2]{3,2,1,0:T(8,128)S(1)}, f32[3,6,12,2]{3,2,1,0:T(8,128)S(1)}, u32[]{:S(2)}, u32[]{:S(2)}) collective-permute-start(f32[3,6,12,2]{3,2,1,0:T(8,128)S(1)} %get-tuple-element.45), channel_id=1, source_target_pairs={{1,0},{2,1},{3,2},{5,4},{6,5},{7,6},{9,8},{10,9},{11,10},{13,12},{... | collective-permute-start | bytes 5192 | tf_op jit(solution)/shard_map/ppermute | solution.py:20
  85.3 2.5 %collective-permute-start.11 = (f32[3,6,12,2]{3,2,1,0:T(8,128)S(1)}, f32[3,6,12,2]{3,2,1,0:T(8,128)S(1)}, u32[]{:S(2)}, u32[]{:S(2)}) collective-permute-start(f32[3,6,12,2]{3,2,1,0:T(8,128)S(1)} %get-tuple-element.44), channel_id=1, source_target_pairs={{0,1},{1,2},{2,3},{4,5},{5,6},{6,7},{8,9},{9,10},{10,11},{12,13},{... | collective-permute-start | bytes 5192 | tf_op jit(solution)/shard_map/ppermute | solution.py:19
  87.9 1.1 collective-permute-done.10
  89.0 3.4 %collective-permute-done.11 = f32[3,6,12,2]{3,2,1,0:T(8,128)S(1)} collective-permute-done((f32[3,6,12,2]{3,2,1,0:T(8,128)S(1)}, f32[3,6,12,2]{3,2,1,0:T(8,128)S(1)}, u32[]{:S(2)}, u32[]{:S(2)}) %collective-permute-start.11) | collective-permute-done | bytes 1760 | tf_op jit(solution)/shard_map/ppermute | solution.py:19
  92.4 0.3 select_maximum_fusion.8
  92.8 0.3 fusion.56
  93.2 1.9 %collective-permute-start.12 = (f32[6,6,2,128]{3,2,1,0:T(2,128)S(1)}, f32[6,6,2,128]{3,2,1,0:T(2,128)S(1)}, u32[]{:S(2)}, u32[]{:S(2)}) collective-permute-start(f32[6,6,2,128]{3,2,1,0:T(2,128)S(1)} %get-tuple-element.43), channel_id=1, source_target_pairs={{4,0},{8,4},{12,8},{16,12},{20,16},{24,20},{28,24},{5,1},{9,5},{13... | collective-permute-start | bytes 110600 | tf_op jit(solution)/shard_map/ppermute | solution.py:20
  95.2 2.4 %collective-permute-start.13 = (f32[6,6,2,128]{3,2,1,0:T(2,128)S(1)}, f32[6,6,2,128]{3,2,1,0:T(2,128)S(1)}, u32[]{:S(2)}, u32[]{:S(2)}) collective-permute-start(f32[6,6,2,128]{3,2,1,0:T(2,128)S(1)} %get-tuple-element.42), channel_id=1, source_target_pairs={{0,4},{4,8},{8,12},{12,16},{16,20},{20,24},{24,28},{1,5},{5,9},{9,... | collective-permute-start | bytes 110600 | tf_op jit(solution)/shard_map/ppermute | solution.py:19
  97.7 1.6 %scatter_custom_fusion.1 = f32[3,1024]{0,1:T(8,128)S(1)} fusion(s32[256]{0:T(256)S(1)} %bitcast.206, f32[256,3]{1,0:T(8,128)S(1)} %bitcast.196, f32[]{:T(128)} %constant.90.clone.1), kind=kCustom, calls=%fused_computation.48 | custom fusion | flops 768 | bytes 12292 | tf_op jit(solution)/shard_map/scatter-add | solution.py:125
  99.5 1.0 collective-permute-done.13
  100.6 3.3 %collective-permute-start.14 = (f32[6,6,12,2]{3,2,1,0:T(8,128)S(1)}, f32[6,6,12,2]{3,2,1,0:T(8,128)S(1)}, u32[]{:S(2)}, u32[]{:S(2)}) collective-permute-start(f32[6,6,12,2]{3,2,1,0:T(8,128)S(1)} %get-tuple-element.39), channel_id=1, source_target_pairs={{1,0},{2,1},{3,2},{5,4},{6,5},{7,6},{9,8},{10,9},{11,10},{13,12},{... | collective-permute-start | bytes 10376 | tf_op jit(solution)/shard_map/ppermute | solution.py:20
  104.0 2.5 %collective-permute-start.15 = (f32[6,6,12,2]{3,2,1,0:T(8,128)S(1)}, f32[6,6,12,2]{3,2,1,0:T(8,128)S(1)}, u32[]{:S(2)}, u32[]{:S(2)}) collective-permute-start(f32[6,6,12,2]{3,2,1,0:T(8,128)S(1)} %get-tuple-element.38), channel_id=1, source_target_pairs={{0,1},{1,2},{2,3},{4,5},{5,6},{6,7},{8,9},{9,10},{10,11},{12,13},{... | collective-permute-start | bytes 10376 | tf_op jit(solution)/shard_map/ppermute | solution.py:19
  106.6 4.9 %collective-permute-done.14 = f32[6,6,12,2]{3,2,1,0:T(8,128)S(1)} collective-permute-done((f32[6,6,12,2]{3,2,1,0:T(8,128)S(1)}, f32[6,6,12,2]{3,2,1,0:T(8,128)S(1)}, u32[]{:S(2)}, u32[]{:S(2)}) %collective-permute-start.14) | collective-permute-done | bytes 3488 | tf_op jit(solution)/shard_map/ppermute | solution.py:20
  111.6 3.1 %collective-permute-done.15 = f32[6,6,12,2]{3,2,1,0:T(8,128)S(1)} collective-permute-done((f32[6,6,12,2]{3,2,1,0:T(8,128)S(1)}, f32[6,6,12,2]{3,2,1,0:T(8,128)S(1)}, u32[]{:S(2)}, u32[]{:S(2)}) %collective-permute-start.15) | collective-permute-done | bytes 3488 | tf_op jit(solution)/shard_map/ppermute | solution.py:19
  114.7 0.5 select_maximum_fusion
  115.1 0.2 fusion.25
  115.3 0.5 fusion.29
  115.9 0.7 multiply_add_fusion
  (102 shorter events, 4.1 us)
Async XLA Ops:
  0.6 14.9 %copy-start = (f32[8,128,128]{2,1,0:T(8,128)S(1)}, f32[8,128,128]{2,1,0:T(8,128)}, u32[]{:S(2)}) copy-start(f32[8,128,128]{2,1,0:T(8,128)} %param.24) | copy-start | bytes 1572868
  0.6 6.6 %copy-start.10 = (f32[8,3,128]{2,0,1:T(8,128)S(1)}, f32[8,3,128]{2,0,1:T(8,128)}, u32[]{:S(2)}) copy-start(f32[8,3,128]{2,0,1:T(8,128)} %param.25) | copy-start | bytes 36868
  1.7 14.6 %collective-permute-start.1 = (f32[3,6,2,128]{3,2,1,0:T(2,128)S(1)}, f32[3,6,2,128]{3,2,1,0:T(2,128)S(1)}, u32[]{:S(2)}, u32[]{:S(2)}) collective-permute-start(f32[3,6,2,128]{3,2,1,0:T(2,128)S(1)} %get-tuple-element.55), channel_id=1, source_target_pairs={{0,4},{4,8},{8,12},{12,16},{16,20},{20,24},{24,28},{1,5},{5,9},{9,... | collective-permute-start | bytes 55304 | tf_op jit(solution)/shard_map/ppermute | solution.py:19
  3.6 12.7 %collective-permute-start = (f32[3,6,2,128]{3,2,1,0:T(2,128)S(1)}, f32[3,6,2,128]{3,2,1,0:T(2,128)S(1)}, u32[]{:S(2)}, u32[]{:S(2)}) collective-permute-start(f32[3,6,2,128]{3,2,1,0:T(2,128)S(1)} %get-tuple-element.54), channel_id=1, source_target_pairs={{4,0},{8,4},{12,8},{16,12},{20,16},{24,20},{28,24},{5,1},{9,5},{13... | collective-permute-start | bytes 55304 | tf_op jit(solution)/shard_map/ppermute | solution.py:20
  7.3 0.8 copy-start.4
  7.3 0.7 copy-start.12
  8.9 15.4 %all-to-all-start = ((f32[3,4,16]{2,0,1:T(4,128)}), f32[3,4,16]{2,0,1:T(4,128)S(1)}, u32[]{:S(2)}, u32[]{:S(2)}) async-start(f32[3,4,16]{2,0,1:T(4,128)} %copy.42), calls=%async_computation | async-start | bytes 16384 | tf_op jit(solution)/shard_map/all_to_all | solution.py:118
  14.9 0.7 copy-start.11
  15.6 0.9 copy-start.2
  16.6 7.8 %collective-permute-start.3 = (f32[3,6,12,2]{3,2,1,0:T(8,128)S(1)}, f32[3,6,12,2]{3,2,1,0:T(8,128)S(1)}, u32[]{:S(2)}, u32[]{:S(2)}) collective-permute-start(f32[3,6,12,2]{3,2,1,0:T(8,128)S(1)} %get-tuple-element.48), channel_id=1, source_target_pairs={{0,1},{1,2},{2,3},{4,5},{5,6},{6,7},{8,9},{9,10},{10,11},{12,13},{... | collective-permute-start | bytes 5192 | tf_op jit(solution)/shard_map/ppermute | solution.py:19
  20.0 7.0 %collective-permute-start.2 = (f32[3,6,12,2]{3,2,1,0:T(8,128)S(1)}, f32[3,6,12,2]{3,2,1,0:T(8,128)S(1)}, u32[]{:S(2)}, u32[]{:S(2)}) collective-permute-start(f32[3,6,12,2]{3,2,1,0:T(8,128)S(1)} %get-tuple-element.49), channel_id=1, source_target_pairs={{1,0},{2,1},{3,2},{5,4},{6,5},{7,6},{9,8},{10,9},{11,10},{13,12},{... | collective-permute-start | bytes 5192 | tf_op jit(solution)/shard_map/ppermute | solution.py:20
  22.4 0.7 slice-start
  27.6 0.7 copy-start.1
  27.6 0.7 copy-start.7
  28.5 6.2 %collective-permute-start.4 = (f32[6,6,2,128]{3,2,1,0:T(2,128)S(1)}, f32[6,6,2,128]{3,2,1,0:T(2,128)S(1)}, u32[]{:S(2)}, u32[]{:S(2)}) collective-permute-start(f32[6,6,2,128]{3,2,1,0:T(2,128)S(1)} %get-tuple-element.47), channel_id=1, source_target_pairs={{4,0},{8,4},{12,8},{16,12},{20,16},{24,20},{28,24},{5,1},{9,5},{13... | collective-permute-start | bytes 110600 | tf_op jit(solution)/shard_map/ppermute | solution.py:20
  30.4 5.3 %collective-permute-start.5 = (f32[6,6,2,128]{3,2,1,0:T(2,128)S(1)}, f32[6,6,2,128]{3,2,1,0:T(2,128)S(1)}, u32[]{:S(2)}, u32[]{:S(2)}) collective-permute-start(f32[6,6,2,128]{3,2,1,0:T(2,128)S(1)} %get-tuple-element.46), channel_id=1, source_target_pairs={{0,4},{4,8},{8,12},{12,16},{16,20},{20,24},{24,28},{1,5},{5,9},{9,... | collective-permute-start | bytes 110600 | tf_op jit(solution)/shard_map/ppermute | solution.py:19
  35.9 11.7 %collective-permute-start.6 = (f32[6,6,12,2]{3,2,1,0:T(8,128)S(1)}, f32[6,6,12,2]{3,2,1,0:T(8,128)S(1)}, u32[]{:S(2)}, u32[]{:S(2)}) collective-permute-start(f32[6,6,12,2]{3,2,1,0:T(8,128)S(1)} %get-tuple-element.41), channel_id=1, source_target_pairs={{1,0},{2,1},{3,2},{5,4},{6,5},{7,6},{9,8},{10,9},{11,10},{13,12},{... | collective-permute-start | bytes 10376 | tf_op jit(solution)/shard_map/ppermute | solution.py:20
  38.3 11.6 %collective-permute-start.7 = (f32[6,6,12,2]{3,2,1,0:T(8,128)S(1)}, f32[6,6,12,2]{3,2,1,0:T(8,128)S(1)}, u32[]{:S(2)}, u32[]{:S(2)}) collective-permute-start(f32[6,6,12,2]{3,2,1,0:T(8,128)S(1)} %get-tuple-element.40), channel_id=1, source_target_pairs={{0,1},{1,2},{2,3},{4,5},{5,6},{6,7},{8,9},{9,10},{10,11},{12,13},{... | collective-permute-start | bytes 10376 | tf_op jit(solution)/shard_map/ppermute | solution.py:19
  51.1 0.9 copy-start.8
  51.2 0.9 copy-start.6
  52.0 63.9 %copy-start.3 = (f32[3,6,8,128]{3,2,1,0:T(8,128)}, f32[3,6,8,128]{3,2,1,0:T(8,128)S(1)}, u32[]{:S(2)}) copy-start(f32[3,6,8,128]{3,2,1,0:T(8,128)S(1)} %multiply_add_fusion.1) | copy-start | bytes 221188
  53.8 10.7 %all-to-all-start.1 = ((f32[3,4,16]{2,0,1:T(4,128)}), f32[3,4,16]{2,0,1:T(4,128)S(1)}, u32[]{:S(2)}, u32[]{:S(2)}) async-start(f32[3,4,16]{2,0,1:T(4,128)} %get-tuple-element.57), calls=%async_computation.1 | async-start | bytes 16384 | tf_op jit(solution)/shard_map/all_to_all | solution.py:114
  58.9 22.9 %collective-permute-start.9 = (f32[3,6,2,128]{3,2,1,0:T(2,128)S(1)}, f32[3,6,2,128]{3,2,1,0:T(2,128)S(1)}, u32[]{:S(2)}, u32[]{:S(2)}) collective-permute-start(f32[3,6,2,128]{3,2,1,0:T(2,128)S(1)} %get-tuple-element.51), channel_id=1, source_target_pairs={{0,4},{4,8},{8,12},{12,16},{16,20},{20,24},{24,28},{1,5},{5,9},{9,... | collective-permute-start | bytes 55304 | tf_op jit(solution)/shard_map/ppermute | solution.py:19
  60.9 20.9 %collective-permute-start.8 = (f32[3,6,2,128]{3,2,1,0:T(2,128)S(1)}, f32[3,6,2,128]{3,2,1,0:T(2,128)S(1)}, u32[]{:S(2)}, u32[]{:S(2)}) collective-permute-start(f32[3,6,2,128]{3,2,1,0:T(2,128)S(1)} %get-tuple-element.50), channel_id=1, source_target_pairs={{4,0},{8,4},{12,8},{16,12},{20,16},{24,20},{28,24},{5,1},{9,5},{13... | collective-permute-start | bytes 55304 | tf_op jit(solution)/shard_map/ppermute | solution.py:20
  64.5 8.4 %all-to-all-start.3 = ((f32[3,4,16]{2,0,1:T(4,128)}), f32[3,4,16]{2,0,1:T(4,128)S(1)}, u32[]{:S(2)}, u32[]{:S(2)}) async-start(f32[3,4,16]{2,0,1:T(4,128)} %get-tuple-element.56), calls=%async_computation.3 | async-start | bytes 16384 | tf_op jit(solution)/shard_map/all_to_all | solution.py:114
  69.7 0.8 copy-start.9
  70.5 8.5 %copy-start.5 = (f32[64,128]{1,0:T(8,128)}, f32[64,128]{1,0:T(8,128)S(1)}, u32[]{:S(2)}) copy-start(f32[64,128]{1,0:T(8,128)S(1)} %multiply_add_fusion.3) | copy-start | bytes 98308
  72.9 8.8 %all-to-all-start.2 = ((f32[3,4,16]{2,0,1:T(4,128)}), f32[3,4,16]{2,0,1:T(4,128)S(1)}, u32[]{:S(2)}, u32[]{:S(2)}) async-start(f32[3,4,16]{2,0,1:T(4,128)} %copy.50), calls=%async_computation.2 | async-start | bytes 16384 | tf_op jit(solution)/shard_map/all_to_all | solution.py:118
  81.9 7.0 %collective-permute-start.10 = (f32[3,6,12,2]{3,2,1,0:T(8,128)S(1)}, f32[3,6,12,2]{3,2,1,0:T(8,128)S(1)}, u32[]{:S(2)}, u32[]{:S(2)}) collective-permute-start(f32[3,6,12,2]{3,2,1,0:T(8,128)S(1)} %get-tuple-element.45), channel_id=1, source_target_pairs={{1,0},{2,1},{3,2},{5,4},{6,5},{7,6},{9,8},{10,9},{11,10},{13,12},{... | collective-permute-start | bytes 5192 | tf_op jit(solution)/shard_map/ppermute | solution.py:20
  85.3 7.0 %collective-permute-start.11 = (f32[3,6,12,2]{3,2,1,0:T(8,128)S(1)}, f32[3,6,12,2]{3,2,1,0:T(8,128)S(1)}, u32[]{:S(2)}, u32[]{:S(2)}) collective-permute-start(f32[3,6,12,2]{3,2,1,0:T(8,128)S(1)} %get-tuple-element.44), channel_id=1, source_target_pairs={{0,1},{1,2},{2,3},{4,5},{5,6},{6,7},{8,9},{9,10},{10,11},{12,13},{... | collective-permute-start | bytes 5192 | tf_op jit(solution)/shard_map/ppermute | solution.py:19
  93.2 6.2 %collective-permute-start.12 = (f32[6,6,2,128]{3,2,1,0:T(2,128)S(1)}, f32[6,6,2,128]{3,2,1,0:T(2,128)S(1)}, u32[]{:S(2)}, u32[]{:S(2)}) collective-permute-start(f32[6,6,2,128]{3,2,1,0:T(2,128)S(1)} %get-tuple-element.43), channel_id=1, source_target_pairs={{4,0},{8,4},{12,8},{16,12},{20,16},{24,20},{28,24},{5,1},{9,5},{13... | collective-permute-start | bytes 110600 | tf_op jit(solution)/shard_map/ppermute | solution.py:20
  95.2 5.3 %collective-permute-start.13 = (f32[6,6,2,128]{3,2,1,0:T(2,128)S(1)}, f32[6,6,2,128]{3,2,1,0:T(2,128)S(1)}, u32[]{:S(2)}, u32[]{:S(2)}) collective-permute-start(f32[6,6,2,128]{3,2,1,0:T(2,128)S(1)} %get-tuple-element.42), channel_id=1, source_target_pairs={{0,4},{4,8},{8,12},{12,16},{16,20},{20,24},{24,28},{1,5},{5,9},{9,... | collective-permute-start | bytes 110600 | tf_op jit(solution)/shard_map/ppermute | solution.py:19
  100.6 11.0 %collective-permute-start.14 = (f32[6,6,12,2]{3,2,1,0:T(8,128)S(1)}, f32[6,6,12,2]{3,2,1,0:T(8,128)S(1)}, u32[]{:S(2)}, u32[]{:S(2)}) collective-permute-start(f32[6,6,12,2]{3,2,1,0:T(8,128)S(1)} %get-tuple-element.39), channel_id=1, source_target_pairs={{1,0},{2,1},{3,2},{5,4},{6,5},{7,6},{9,8},{10,9},{11,10},{13,12},{... | collective-permute-start | bytes 10376 | tf_op jit(solution)/shard_map/ppermute | solution.py:20
  104.0 10.7 %collective-permute-start.15 = (f32[6,6,12,2]{3,2,1,0:T(8,128)S(1)}, f32[6,6,12,2]{3,2,1,0:T(8,128)S(1)}, u32[]{:S(2)}, u32[]{:S(2)}) collective-permute-start(f32[6,6,12,2]{3,2,1,0:T(8,128)S(1)} %get-tuple-element.38), channel_id=1, source_target_pairs={{0,1},{1,2},{2,3},{4,5},{5,6},{6,7},{8,9},{9,10},{10,11},{12,13},{... | collective-permute-start | bytes 10376 | tf_op jit(solution)/shard_map/ppermute | solution.py:19
where the time goes:
time: 118 us; the launch traced here: 117 us
  starting transfers between devices  64.1 us (54%)
  waiting for transfers between devices  28 us (24%)
  local copies, waits for them, and re-layouts  10.7 us (9%)
  other arithmetic  9.77 us (8%)
  matrix products  2.55 us (2%)
  between operations  1.33 us (1%)
    ppermute x8, starting transfers between devices, with_halo(): after = lax.ppermute(initial, axis, down)  22.8 us
    ppermute x8, starting transfers between devices, with_halo(): before = lax.ppermute(last, axis, up)  20.4 us
    ppermute x8, waiting for transfers between devices, with_halo(): after = lax.ppermute(initial, axis, down)  14.3 us
    ppermute x8, waiting for transfers between devices, with_halo(): before = lax.ppermute(last, axis, up)  10.8 us
    all_to_all x2, starting transfers between devices, shards(): lax.all_to_all(shear_force.T, 'gy', split_axis=1, concat_axis=1, tiled=True)  10.8 us
    all_to_all x2, starting transfers between devices, shards(): lax.all_to_all(base_layer, 'gy', split_axis=1, concat_axis=1, tiled=True)  10.2 us
    unnamed x26, local copies, waits for them, and re-layouts  3.3 us
    scatter-add x2, other arithmetic, shards(): force = jnp.zeros((3, cells_x * cells_y), jnp.float32).at[:, cells].add(c...  3.1 us
  transfers between devices with their start and end apart: 20, of which 11 were waited for; matrix products, arithmetic and copies ran while one was open for 9% of the time, Pallas kernels for 0%

commit v1 on v0

--- a/solution.py
+++ b/solution.py
@@ -115,7 +115,15 @@
         shear_all = jnp.dot(frame_state, shear_table, precision=highest).reshape(slots, kinds, 3)
         shear_force = jnp.sum(shear_all * onehot[:, :, None], axis=1)
         returned = (
-            lax.all_to_all(shear_force.T, "gy", split_axis=1, concat_axis=1, tiled=True)
+            jnp.concatenate(
+                lax.all_to_all(
+                    jnp.stack(jnp.split(shear_force.T, lax.axis_size("gy"), axis=1), axis=0),
+                    axis_name="gy",
+                    split_axis=0,
+                    concat_axis=0,
+                ),
+                axis=1,
+            )
             * active_slots
         )
         contrib = jnp.repeat(returned / FOOTPRINT_CELLS, FOOTPRINT_CELLS, axis=1)

time: 118 us -> 118 us (level)
  other arithmetic: 9.77 us -> 11 us
  local copies, waits for them, and re-layouts: 10.7 us -> 9.47 us
    all_to_all x8 -> x0, local copies, waits for them, and re-layouts: 1.57 us -> none  [shards(): lax.all_to_all(shear_force.T, 'gy', split_axis=1, concat_axis=1, tiled=True)]
    another operation x0 -> x2, other arithmetic: none -> 1.22 us  [shards(): jnp.stack(jnp.split(shear_force.T, lax.axis_size('gy'), axis=1), axis=0)]
  transfers between devices with their start and end apart: 20 -> 20, of which waited for: 11 -> 11; matrix products, arithmetic and copies ran while one was open for 9% -> 10% of each run, Pallas kernels for 0% -> 0%
where the time goes in v1:
time: 118 us; the launch traced here: 117 us
  starting transfers between devices  64.1 us (54%)
  waiting for transfers between devices  28.1 us (24%)
  other arithmetic  11 us (9%)
  local copies, waits for them, and re-layouts  9.47 us (8%)
  matrix products  2.55 us (2%)
  between operations  1.33 us (1%)
    ppermute x8, starting transfers between devices, with_halo(): after = lax.ppermute(initial, axis, down)  22.8 us
    ppermute x8, starting transfers between devices, with_halo(): before = lax.ppermute(last, axis, up)  20.4 us
    ppermute x8, waiting for transfers between devices, with_halo(): after = lax.ppermute(initial, axis, down)  14.3 us
    ppermute x8, waiting for transfers between devices, with_halo(): before = lax.ppermute(last, axis, up)  10.8 us
    all_to_all x2, starting transfers between devices, shards(): lax.all_to_all(jnp.stack(jnp.split(shear_force.T, lax.axis_size('gy'), ax...  10.8 us
    all_to_all x2, starting transfers between devices, shards(): lax.all_to_all(base_layer, 'gy', split_axis=1, concat_axis=1, tiled=True)  10.2 us
    unnamed x26, local copies, waits for them, and re-layouts  3.3 us
    scatter-add x2, other arithmetic, shards(): force = jnp.zeros((3, cells_x * cells_y), jnp.float32).at[:, cells].add(c...  3.1 us
  transfers between devices with their start and end apart: 20, of which 11 were waited for; matrix products, arithmetic and copies ran while one was open for 10% of the time, Pallas kernels for 0%

profile of v1, /device:TPU:18, one launch (start us, length us, event | category | flops | bytes accessed | tf_op | source)
XLA Modules:
  0.0 116.6 jit_solution(2574577545395764249)
XLA Ops:
  0.7 1.0 fusion.106
  1.7 1.9 %collective-permute-start.1 = (f32[3,6,2,128]{3,2,1,0:T(2,128)S(1)}, f32[3,6,2,128]{3,2,1,0:T(2,128)S(1)}, u32[]{:S(2)}, u32[]{:S(2)}) collective-permute-start(f32[3,6,2,128]{3,2,1,0:T(2,128)S(1)} %get-tuple-element.55), channel_id=1, source_target_pairs={{0,4},{4,8},{8,12},{12,16},{16,20},{20,24},{24,28},{1,5},{5,9},{9,... | collective-permute-start | bytes 55304 | tf_op jit(solution)/shard_map/ppermute | solution.py:19
  3.6 3.6 %collective-permute-start = (f32[3,6,2,128]{3,2,1,0:T(2,128)S(1)}, f32[3,6,2,128]{3,2,1,0:T(2,128)S(1)}, u32[]{:S(2)}, u32[]{:S(2)}) collective-permute-start(f32[3,6,2,128]{3,2,1,0:T(2,128)S(1)} %get-tuple-element.54), channel_id=1, source_target_pairs={{4,0},{8,4},{12,8},{16,12},{20,16},{24,20},{28,24},{5,1},{9,5},{13... | collective-permute-start | bytes 55304 | tf_op jit(solution)/shard_map/ppermute | solution.py:20
  7.3 0.6 copy-done.12
  8.3 0.6 pad_maximum_fusion.37
  8.9 5.2 %all-to-all-start = ((f32[4,3,16]{2,1,0:T(4,128)}), f32[4,3,16]{2,1,0:T(4,128)S(1)}, u32[]{:S(2)}, u32[]{:S(2)}) async-start(f32[4,3,16]{2,1,0:T(4,128)} %pad_maximum_fusion.37), calls=%async_computation | async-start | bytes 16384 | tf_op jit(solution)/shard_map/all_to_all | solution.py:119
  14.1 0.7 fusion.98
  14.9 0.6 copy-done.11
  15.5 0.7 fusion.2
  16.6 3.4 %collective-permute-start.3 = (f32[3,6,12,2]{3,2,1,0:T(8,128)S(1)}, f32[3,6,12,2]{3,2,1,0:T(8,128)S(1)}, u32[]{:S(2)}, u32[]{:S(2)}) collective-permute-start(f32[3,6,12,2]{3,2,1,0:T(8,128)S(1)} %get-tuple-element.48), channel_id=1, source_target_pairs={{0,1},{1,2},{2,3},{4,5},{5,6},{6,7},{8,9},{9,10},{10,11},{12,13},{... | collective-permute-start | bytes 5192 | tf_op jit(solution)/shard_map/ppermute | solution.py:19
  19.9 2.5 %collective-permute-start.2 = (f32[3,6,12,2]{3,2,1,0:T(8,128)S(1)}, f32[3,6,12,2]{3,2,1,0:T(8,128)S(1)}, u32[]{:S(2)}, u32[]{:S(2)}) collective-permute-start(f32[3,6,12,2]{3,2,1,0:T(8,128)S(1)} %get-tuple-element.49), channel_id=1, source_target_pairs={{1,0},{2,1},{3,2},{5,4},{6,5},{7,6},{9,8},{10,9},{11,10},{13,12},{... | collective-permute-start | bytes 5192 | tf_op jit(solution)/shard_map/ppermute | solution.py:20
  22.5 0.6 slice-done
  23.2 0.2 copy.36
  23.4 0.7 gather_fusion
  24.4 2.6 %collective-permute-done.2 = f32[3,6,12,2]{3,2,1,0:T(8,128)S(1)} collective-permute-done((f32[3,6,12,2]{3,2,1,0:T(8,128)S(1)}, f32[3,6,12,2]{3,2,1,0:T(8,128)S(1)}, u32[]{:S(2)}, u32[]{:S(2)}) %collective-permute-start.2) | collective-permute-done | bytes 1760 | tf_op jit(solution)/shard_map/ppermute | solution.py:20
  27.0 0.3 fusion.64
  27.3 0.3 select_maximum_fusion.12
  27.7 0.6 copy-done.1
  28.4 1.9 %collective-permute-start.4 = (f32[6,6,2,128]{3,2,1,0:T(2,128)S(1)}, f32[6,6,2,128]{3,2,1,0:T(2,128)S(1)}, u32[]{:S(2)}, u32[]{:S(2)}) collective-permute-start(f32[6,6,2,128]{3,2,1,0:T(2,128)S(1)} %get-tuple-element.47), channel_id=1, source_target_pairs={{4,0},{8,4},{12,8},{16,12},{20,16},{24,20},{28,24},{5,1},{9,5},{13... | collective-permute-start | bytes 110600 | tf_op jit(solution)/shard_map/ppermute | solution.py:20
  30.4 2.4 %collective-permute-start.5 = (f32[6,6,2,128]{3,2,1,0:T(2,128)S(1)}, f32[6,6,2,128]{3,2,1,0:T(2,128)S(1)}, u32[]{:S(2)}, u32[]{:S(2)}) collective-permute-start(f32[6,6,2,128]{3,2,1,0:T(2,128)S(1)} %get-tuple-element.46), channel_id=1, source_target_pairs={{0,4},{4,8},{8,12},{12,16},{16,20},{20,24},{24,28},{1,5},{5,9},{9,... | collective-permute-start | bytes 110600 | tf_op jit(solution)/shard_map/ppermute | solution.py:19
  32.9 1.6 %scatter_custom_fusion = f32[3,1024]{0,1:T(8,128)S(1)} fusion(s32[256]{0:T(256)S(1)} %bitcast.225, f32[256,3]{1,0:T(8,128)S(1)} %bitcast.215, f32[]{:T(128)} %constant.90.clone.1), kind=kCustom, calls=%fused_computation.50 | custom fusion | flops 768 | bytes 12292 | tf_op jit(solution)/shard_map/scatter-add | solution.py:133
  34.7 1.0 collective-permute-done.5
  35.9 2.5 %collective-permute-start.6 = (f32[6,6,12,2]{3,2,1,0:T(8,128)S(1)}, f32[6,6,12,2]{3,2,1,0:T(8,128)S(1)}, u32[]{:S(2)}, u32[]{:S(2)}) collective-permute-start(f32[6,6,12,2]{3,2,1,0:T(8,128)S(1)} %get-tuple-element.41), channel_id=1, source_target_pairs={{1,0},{2,1},{3,2},{5,4},{6,5},{7,6},{9,8},{10,9},{11,10},{13,12},{... | collective-permute-start | bytes 10376 | tf_op jit(solution)/shard_map/ppermute | solution.py:20
  38.3 3.4 %collective-permute-start.7 = (f32[6,6,12,2]{3,2,1,0:T(8,128)S(1)}, f32[6,6,12,2]{3,2,1,0:T(8,128)S(1)}, u32[]{:S(2)}, u32[]{:S(2)}) collective-permute-start(f32[6,6,12,2]{3,2,1,0:T(8,128)S(1)} %get-tuple-element.40), channel_id=1, source_target_pairs={{0,1},{1,2},{2,3},{4,5},{5,6},{6,7},{8,9},{9,10},{10,11},{12,13},{... | collective-permute-start | bytes 10376 | tf_op jit(solution)/shard_map/ppermute | solution.py:19
  41.9 5.7 %collective-permute-done.6 = f32[6,6,12,2]{3,2,1,0:T(8,128)S(1)} collective-permute-done((f32[6,6,12,2]{3,2,1,0:T(8,128)S(1)}, f32[6,6,12,2]{3,2,1,0:T(8,128)S(1)}, u32[]{:S(2)}, u32[]{:S(2)}) %collective-permute-start.6) | collective-permute-done | bytes 3488 | tf_op jit(solution)/shard_map/ppermute | solution.py:20
  47.6 2.3 %collective-permute-done.7 = f32[6,6,12,2]{3,2,1,0:T(8,128)S(1)} collective-permute-done((f32[6,6,12,2]{3,2,1,0:T(8,128)S(1)}, f32[6,6,12,2]{3,2,1,0:T(8,128)S(1)}, u32[]{:S(2)}, u32[]{:S(2)}) %collective-permute-start.7) | collective-permute-done | bytes 3488 | tf_op jit(solution)/shard_map/ppermute | solution.py:19
  49.9 0.5 select_maximum_fusion.4
  50.4 0.2 fusion.33
  50.6 0.5 fusion.37
  51.2 0.8 copy-done.8
  52.1 0.2 copy.43
  52.3 0.7 gather_fusion.1
  53.2 0.6 broadcast_multiply_fusion
  53.8 5.1 %all-to-all-start.1 = ((f32[3,4,16]{2,0,1:T(4,128)}), f32[3,4,16]{2,0,1:T(4,128)S(1)}, u32[]{:S(2)}, u32[]{:S(2)}) async-start(f32[3,4,16]{2,0,1:T(4,128)} %get-tuple-element.57), calls=%async_computation.1 | async-start | bytes 16384 | tf_op jit(solution)/shard_map/all_to_all | solution.py:114
  58.9 1.9 %collective-permute-start.9 = (f32[3,6,2,128]{3,2,1,0:T(2,128)S(1)}, f32[3,6,2,128]{3,2,1,0:T(2,128)S(1)}, u32[]{:S(2)}, u32[]{:S(2)}) collective-permute-start(f32[3,6,2,128]{3,2,1,0:T(2,128)S(1)} %get-tuple-element.51), channel_id=1, source_target_pairs={{0,4},{4,8},{8,12},{12,16},{16,20},{20,24},{24,28},{1,5},{5,9},{9,... | collective-permute-start | bytes 55304 | tf_op jit(solution)/shard_map/ppermute | solution.py:19
  60.9 3.6 %collective-permute-start.8 = (f32[3,6,2,128]{3,2,1,0:T(2,128)S(1)}, f32[3,6,2,128]{3,2,1,0:T(2,128)S(1)}, u32[]{:S(2)}, u32[]{:S(2)}) collective-permute-start(f32[3,6,2,128]{3,2,1,0:T(2,128)S(1)} %get-tuple-element.50), channel_id=1, source_target_pairs={{4,0},{8,4},{12,8},{16,12},{20,16},{24,20},{28,24},{5,1},{9,5},{13... | collective-permute-start | bytes 55304 | tf_op jit(solution)/shard_map/ppermute | solution.py:20
  64.5 5.1 %all-to-all-start.3 = ((f32[3,4,16]{2,0,1:T(4,128)}), f32[3,4,16]{2,0,1:T(4,128)S(1)}, u32[]{:S(2)}, u32[]{:S(2)}) async-start(f32[3,4,16]{2,0,1:T(4,128)} %get-tuple-element.56), calls=%async_computation.3 | async-start | bytes 16384 | tf_op jit(solution)/shard_map/all_to_all | solution.py:114
  69.7 0.4 fusion
  70.2 0.3 copy-done.9
  70.7 0.7 fusion.3
  71.4 0.6 pad_maximum_fusion.38
  72.0 0.8 all-to-all-done.3
  72.9 5.6 %all-to-all-start.2 = ((f32[4,3,16]{2,1,0:T(4,128)}), f32[4,3,16]{2,1,0:T(4,128)S(1)}, u32[]{:S(2)}, u32[]{:S(2)}) async-start(f32[4,3,16]{2,1,0:T(4,128)} %pad_maximum_fusion.38), calls=%async_computation.2 | async-start | bytes 16384 | tf_op jit(solution)/shard_map/all_to_all | solution.py:119
  78.5 0.4 fusion.1
  79.0 0.6 multiply_add_fusion.2
  79.6 2.1 %all-to-all-done.2 = f32[4,3,16]{2,1,0:T(4,128)S(1)} async-done(((f32[4,3,16]{2,1,0:T(4,128)}), f32[4,3,16]{2,1,0:T(4,128)S(1)}, u32[]{:S(2)}, u32[]{:S(2)}) %all-to-all-start.2) | async-done | bytes 800 | tf_op jit(solution)/shard_map/all_to_all | solution.py:119
  81.9 3.4 %collective-permute-start.10 = (f32[3,6,12,2]{3,2,1,0:T(8,128)S(1)}, f32[3,6,12,2]{3,2,1,0:T(8,128)S(1)}, u32[]{:S(2)}, u32[]{:S(2)}) collective-permute-start(f32[3,6,12,2]{3,2,1,0:T(8,128)S(1)} %get-tuple-element.45), channel_id=1, source_target_pairs={{1,0},{2,1},{3,2},{5,4},{6,5},{7,6},{9,8},{10,9},{11,10},{13,12},{... | collective-permute-start | bytes 5192 | tf_op jit(solution)/shard_map/ppermute | solution.py:20
  85.3 2.5 %collective-permute-start.11 = (f32[3,6,12,2]{3,2,1,0:T(8,128)S(1)}, f32[3,6,12,2]{3,2,1,0:T(8,128)S(1)}, u32[]{:S(2)}, u32[]{:S(2)}) collective-permute-start(f32[3,6,12,2]{3,2,1,0:T(8,128)S(1)} %get-tuple-element.44), channel_id=1, source_target_pairs={{0,1},{1,2},{2,3},{4,5},{5,6},{6,7},{8,9},{9,10},{10,11},{12,13},{... | collective-permute-start | bytes 5192 | tf_op jit(solution)/shard_map/ppermute | solution.py:19
  87.9 1.1 collective-permute-done.10
  89.0 3.4 %collective-permute-done.11 = f32[3,6,12,2]{3,2,1,0:T(8,128)S(1)} collective-permute-done((f32[3,6,12,2]{3,2,1,0:T(8,128)S(1)}, f32[3,6,12,2]{3,2,1,0:T(8,128)S(1)}, u32[]{:S(2)}, u32[]{:S(2)}) %collective-permute-start.11) | collective-permute-done | bytes 1760 | tf_op jit(solution)/shard_map/ppermute | solution.py:19
  92.4 0.3 select_maximum_fusion.8
  92.8 0.3 fusion.56
  93.2 1.9 %collective-permute-start.12 = (f32[6,6,2,128]{3,2,1,0:T(2,128)S(1)}, f32[6,6,2,128]{3,2,1,0:T(2,128)S(1)}, u32[]{:S(2)}, u32[]{:S(2)}) collective-permute-start(f32[6,6,2,128]{3,2,1,0:T(2,128)S(1)} %get-tuple-element.43), channel_id=1, source_target_pairs={{4,0},{8,4},{12,8},{16,12},{20,16},{24,20},{28,24},{5,1},{9,5},{13... | collective-permute-start | bytes 110600 | tf_op jit(solution)/shard_map/ppermute | solution.py:20
  95.1 2.4 %collective-permute-start.13 = (f32[6,6,2,128]{3,2,1,0:T(2,128)S(1)}, f32[6,6,2,128]{3,2,1,0:T(2,128)S(1)}, u32[]{:S(2)}, u32[]{:S(2)}) collective-permute-start(f32[6,6,2,128]{3,2,1,0:T(2,128)S(1)} %get-tuple-element.42), channel_id=1, source_target_pairs={{0,4},{4,8},{8,12},{12,16},{16,20},{20,24},{24,28},{1,5},{5,9},{9,... | collective-permute-start | bytes 110600 | tf_op jit(solution)/shard_map/ppermute | solution.py:19
  97.7 1.6 %scatter_custom_fusion.1 = f32[3,1024]{0,1:T(8,128)S(1)} fusion(s32[256]{0:T(256)S(1)} %bitcast.226, f32[256,3]{1,0:T(8,128)S(1)} %bitcast.214, f32[]{:T(128)} %constant.90.clone.1), kind=kCustom, calls=%fused_computation.48 | custom fusion | flops 768 | bytes 12292 | tf_op jit(solution)/shard_map/scatter-add | solution.py:133
  99.4 1.0 collective-permute-done.13
  100.6 3.3 %collective-permute-start.14 = (f32[6,6,12,2]{3,2,1,0:T(8,128)S(1)}, f32[6,6,12,2]{3,2,1,0:T(8,128)S(1)}, u32[]{:S(2)}, u32[]{:S(2)}) collective-permute-start(f32[6,6,12,2]{3,2,1,0:T(8,128)S(1)} %get-tuple-element.39), channel_id=1, source_target_pairs={{1,0},{2,1},{3,2},{5,4},{6,5},{7,6},{9,8},{10,9},{11,10},{13,12},{... | collective-permute-start | bytes 10376 | tf_op jit(solution)/shard_map/ppermute | solution.py:20
  104.0 2.5 %collective-permute-start.15 = (f32[6,6,12,2]{3,2,1,0:T(8,128)S(1)}, f32[6,6,12,2]{3,2,1,0:T(8,128)S(1)}, u32[]{:S(2)}, u32[]{:S(2)}) collective-permute-start(f32[6,6,12,2]{3,2,1,0:T(8,128)S(1)} %get-tuple-element.38), channel_id=1, source_target_pairs={{0,1},{1,2},{2,3},{4,5},{5,6},{6,7},{8,9},{9,10},{10,11},{12,13},{... | collective-permute-start | bytes 10376 | tf_op jit(solution)/shard_map/ppermute | solution.py:19
  106.6 4.9 %collective-permute-done.14 = f32[6,6,12,2]{3,2,1,0:T(8,128)S(1)} collective-permute-done((f32[6,6,12,2]{3,2,1,0:T(8,128)S(1)}, f32[6,6,12,2]{3,2,1,0:T(8,128)S(1)}, u32[]{:S(2)}, u32[]{:S(2)}) %collective-permute-start.14) | collective-permute-done | bytes 3488 | tf_op jit(solution)/shard_map/ppermute | solution.py:20
  111.6 3.1 %collective-permute-done.15 = f32[6,6,12,2]{3,2,1,0:T(8,128)S(1)} collective-permute-done((f32[6,6,12,2]{3,2,1,0:T(8,128)S(1)}, f32[6,6,12,2]{3,2,1,0:T(8,128)S(1)}, u32[]{:S(2)}, u32[]{:S(2)}) %collective-permute-start.15) | collective-permute-done | bytes 3488 | tf_op jit(solution)/shard_map/ppermute | solution.py:19
  114.6 0.5 select_maximum_fusion
  115.1 0.2 fusion.25
  115.3 0.5 fusion.29
  115.9 0.7 multiply_add_fusion
  (102 shorter events, 4.0 us)
Async XLA Ops:
  0.6 14.9 %copy-start = (f32[8,128,128]{2,1,0:T(8,128)S(1)}, f32[8,128,128]{2,1,0:T(8,128)}, u32[]{:S(2)}) copy-start(f32[8,128,128]{2,1,0:T(8,128)} %param.24) | copy-start | bytes 1572868
  0.6 6.6 %copy-start.10 = (f32[8,3,128]{2,0,1:T(8,128)S(1)}, f32[8,3,128]{2,0,1:T(8,128)}, u32[]{:S(2)}) copy-start(f32[8,3,128]{2,0,1:T(8,128)} %param.25) | copy-start | bytes 36868
  1.7 14.6 %collective-permute-start.1 = (f32[3,6,2,128]{3,2,1,0:T(2,128)S(1)}, f32[3,6,2,128]{3,2,1,0:T(2,128)S(1)}, u32[]{:S(2)}, u32[]{:S(2)}) collective-permute-start(f32[3,6,2,128]{3,2,1,0:T(2,128)S(1)} %get-tuple-element.55), channel_id=1, source_target_pairs={{0,4},{4,8},{8,12},{12,16},{16,20},{20,24},{24,28},{1,5},{5,9},{9,... | collective-permute-start | bytes 55304 | tf_op jit(solution)/shard_map/ppermute | solution.py:19
  3.6 12.6 %collective-permute-start = (f32[3,6,2,128]{3,2,1,0:T(2,128)S(1)}, f32[3,6,2,128]{3,2,1,0:T(2,128)S(1)}, u32[]{:S(2)}, u32[]{:S(2)}) collective-permute-start(f32[3,6,2,128]{3,2,1,0:T(2,128)S(1)} %get-tuple-element.54), channel_id=1, source_target_pairs={{4,0},{8,4},{12,8},{16,12},{20,16},{24,20},{28,24},{5,1},{9,5},{13... | collective-permute-start | bytes 55304 | tf_op jit(solution)/shard_map/ppermute | solution.py:20
  7.3 0.8 copy-start.4
  7.3 0.7 copy-start.12
  8.9 15.4 %all-to-all-start = ((f32[4,3,16]{2,1,0:T(4,128)}), f32[4,3,16]{2,1,0:T(4,128)S(1)}, u32[]{:S(2)}, u32[]{:S(2)}) async-start(f32[4,3,16]{2,1,0:T(4,128)} %pad_maximum_fusion.37), calls=%async_computation | async-start | bytes 16384 | tf_op jit(solution)/shard_map/all_to_all | solution.py:119
  14.9 0.7 copy-start.11
  15.5 0.9 copy-start.2
  16.6 7.8 %collective-permute-start.3 = (f32[3,6,12,2]{3,2,1,0:T(8,128)S(1)}, f32[3,6,12,2]{3,2,1,0:T(8,128)S(1)}, u32[]{:S(2)}, u32[]{:S(2)}) collective-permute-start(f32[3,6,12,2]{3,2,1,0:T(8,128)S(1)} %get-tuple-element.48), channel_id=1, source_target_pairs={{0,1},{1,2},{2,3},{4,5},{5,6},{6,7},{8,9},{9,10},{10,11},{12,13},{... | collective-permute-start | bytes 5192 | tf_op jit(solution)/shard_map/ppermute | solution.py:19
  19.9 7.0 %collective-permute-start.2 = (f32[3,6,12,2]{3,2,1,0:T(8,128)S(1)}, f32[3,6,12,2]{3,2,1,0:T(8,128)S(1)}, u32[]{:S(2)}, u32[]{:S(2)}) collective-permute-start(f32[3,6,12,2]{3,2,1,0:T(8,128)S(1)} %get-tuple-element.49), channel_id=1, source_target_pairs={{1,0},{2,1},{3,2},{5,4},{6,5},{7,6},{9,8},{10,9},{11,10},{13,12},{... | collective-permute-start | bytes 5192 | tf_op jit(solution)/shard_map/ppermute | solution.py:20
  22.4 0.7 slice-start
  27.6 0.7 copy-start.1
  27.6 0.7 copy-start.7
  28.4 6.2 %collective-permute-start.4 = (f32[6,6,2,128]{3,2,1,0:T(2,128)S(1)}, f32[6,6,2,128]{3,2,1,0:T(2,128)S(1)}, u32[]{:S(2)}, u32[]{:S(2)}) collective-permute-start(f32[6,6,2,128]{3,2,1,0:T(2,128)S(1)} %get-tuple-element.47), channel_id=1, source_target_pairs={{4,0},{8,4},{12,8},{16,12},{20,16},{24,20},{28,24},{5,1},{9,5},{13... | collective-permute-start | bytes 110600 | tf_op jit(solution)/shard_map/ppermute | solution.py:20
  30.4 5.3 %collective-permute-start.5 = (f32[6,6,2,128]{3,2,1,0:T(2,128)S(1)}, f32[6,6,2,128]{3,2,1,0:T(2,128)S(1)}, u32[]{:S(2)}, u32[]{:S(2)}) collective-permute-start(f32[6,6,2,128]{3,2,1,0:T(2,128)S(1)} %get-tuple-element.46), channel_id=1, source_target_pairs={{0,4},{4,8},{8,12},{12,16},{16,20},{20,24},{24,28},{1,5},{5,9},{9,... | collective-permute-start | bytes 110600 | tf_op jit(solution)/shard_map/ppermute | solution.py:19
  35.9 11.7 %collective-permute-start.6 = (f32[6,6,12,2]{3,2,1,0:T(8,128)S(1)}, f32[6,6,12,2]{3,2,1,0:T(8,128)S(1)}, u32[]{:S(2)}, u32[]{:S(2)}) collective-permute-start(f32[6,6,12,2]{3,2,1,0:T(8,128)S(1)} %get-tuple-element.41), channel_id=1, source_target_pairs={{1,0},{2,1},{3,2},{5,4},{6,5},{7,6},{9,8},{10,9},{11,10},{13,12},{... | collective-permute-start | bytes 10376 | tf_op jit(solution)/shard_map/ppermute | solution.py:20
  38.3 11.6 %collective-permute-start.7 = (f32[6,6,12,2]{3,2,1,0:T(8,128)S(1)}, f32[6,6,12,2]{3,2,1,0:T(8,128)S(1)}, u32[]{:S(2)}, u32[]{:S(2)}) collective-permute-start(f32[6,6,12,2]{3,2,1,0:T(8,128)S(1)} %get-tuple-element.40), channel_id=1, source_target_pairs={{0,1},{1,2},{2,3},{4,5},{5,6},{6,7},{8,9},{9,10},{10,11},{12,13},{... | collective-permute-start | bytes 10376 | tf_op jit(solution)/shard_map/ppermute | solution.py:19
  51.1 0.9 copy-start.8
  51.2 0.9 copy-start.6
  52.0 63.9 %copy-start.3 = (f32[3,6,8,128]{3,2,1,0:T(8,128)}, f32[3,6,8,128]{3,2,1,0:T(8,128)S(1)}, u32[]{:S(2)}) copy-start(f32[3,6,8,128]{3,2,1,0:T(8,128)S(1)} %multiply_add_fusion.1) | copy-start | bytes 221188
  53.8 10.7 %all-to-all-start.1 = ((f32[3,4,16]{2,0,1:T(4,128)}), f32[3,4,16]{2,0,1:T(4,128)S(1)}, u32[]{:S(2)}, u32[]{:S(2)}) async-start(f32[3,4,16]{2,0,1:T(4,128)} %get-tuple-element.57), calls=%async_computation.1 | async-start | bytes 16384 | tf_op jit(solution)/shard_map/all_to_all | solution.py:114
  58.9 22.9 %collective-permute-start.9 = (f32[3,6,2,128]{3,2,1,0:T(2,128)S(1)}, f32[3,6,2,128]{3,2,1,0:T(2,128)S(1)}, u32[]{:S(2)}, u32[]{:S(2)}) collective-permute-start(f32[3,6,2,128]{3,2,1,0:T(2,128)S(1)} %get-tuple-element.51), channel_id=1, source_target_pairs={{0,4},{4,8},{8,12},{12,16},{16,20},{20,24},{24,28},{1,5},{5,9},{9,... | collective-permute-start | bytes 55304 | tf_op jit(solution)/shard_map/ppermute | solution.py:19
  60.9 20.9 %collective-permute-start.8 = (f32[3,6,2,128]{3,2,1,0:T(2,128)S(1)}, f32[3,6,2,128]{3,2,1,0:T(2,128)S(1)}, u32[]{:S(2)}, u32[]{:S(2)}) collective-permute-start(f32[3,6,2,128]{3,2,1,0:T(2,128)S(1)} %get-tuple-element.50), channel_id=1, source_target_pairs={{4,0},{8,4},{12,8},{16,12},{20,16},{24,20},{28,24},{5,1},{9,5},{13... | collective-permute-start | bytes 55304 | tf_op jit(solution)/shard_map/ppermute | solution.py:20
  64.5 8.4 %all-to-all-start.3 = ((f32[3,4,16]{2,0,1:T(4,128)}), f32[3,4,16]{2,0,1:T(4,128)S(1)}, u32[]{:S(2)}, u32[]{:S(2)}) async-start(f32[3,4,16]{2,0,1:T(4,128)} %get-tuple-element.56), calls=%async_computation.3 | async-start | bytes 16384 | tf_op jit(solution)/shard_map/all_to_all | solution.py:114
  69.7 0.8 copy-start.9
  70.5 8.5 %copy-start.5 = (f32[64,128]{1,0:T(8,128)}, f32[64,128]{1,0:T(8,128)S(1)}, u32[]{:S(2)}) copy-start(f32[64,128]{1,0:T(8,128)S(1)} %multiply_add_fusion.3) | copy-start | bytes 98308
  72.9 8.8 %all-to-all-start.2 = ((f32[4,3,16]{2,1,0:T(4,128)}), f32[4,3,16]{2,1,0:T(4,128)S(1)}, u32[]{:S(2)}, u32[]{:S(2)}) async-start(f32[4,3,16]{2,1,0:T(4,128)} %pad_maximum_fusion.38), calls=%async_computation.2 | async-start | bytes 16384 | tf_op jit(solution)/shard_map/all_to_all | solution.py:119
  81.9 7.0 %collective-permute-start.10 = (f32[3,6,12,2]{3,2,1,0:T(8,128)S(1)}, f32[3,6,12,2]{3,2,1,0:T(8,128)S(1)}, u32[]{:S(2)}, u32[]{:S(2)}) collective-permute-start(f32[3,6,12,2]{3,2,1,0:T(8,128)S(1)} %get-tuple-element.45), channel_id=1, source_target_pairs={{1,0},{2,1},{3,2},{5,4},{6,5},{7,6},{9,8},{10,9},{11,10},{13,12},{... | collective-permute-start | bytes 5192 | tf_op jit(solution)/shard_map/ppermute | solution.py:20
  85.3 7.0 %collective-permute-start.11 = (f32[3,6,12,2]{3,2,1,0:T(8,128)S(1)}, f32[3,6,12,2]{3,2,1,0:T(8,128)S(1)}, u32[]{:S(2)}, u32[]{:S(2)}) collective-permute-start(f32[3,6,12,2]{3,2,1,0:T(8,128)S(1)} %get-tuple-element.44), channel_id=1, source_target_pairs={{0,1},{1,2},{2,3},{4,5},{5,6},{6,7},{8,9},{9,10},{10,11},{12,13},{... | collective-permute-start | bytes 5192 | tf_op jit(solution)/shard_map/ppermute | solution.py:19
  93.2 6.2 %collective-permute-start.12 = (f32[6,6,2,128]{3,2,1,0:T(2,128)S(1)}, f32[6,6,2,128]{3,2,1,0:T(2,128)S(1)}, u32[]{:S(2)}, u32[]{:S(2)}) collective-permute-start(f32[6,6,2,128]{3,2,1,0:T(2,128)S(1)} %get-tuple-element.43), channel_id=1, source_target_pairs={{4,0},{8,4},{12,8},{16,12},{20,16},{24,20},{28,24},{5,1},{9,5},{13... | collective-permute-start | bytes 110600 | tf_op jit(solution)/shard_map/ppermute | solution.py:20
  95.1 5.3 %collective-permute-start.13 = (f32[6,6,2,128]{3,2,1,0:T(2,128)S(1)}, f32[6,6,2,128]{3,2,1,0:T(2,128)S(1)}, u32[]{:S(2)}, u32[]{:S(2)}) collective-permute-start(f32[6,6,2,128]{3,2,1,0:T(2,128)S(1)} %get-tuple-element.42), channel_id=1, source_target_pairs={{0,4},{4,8},{8,12},{12,16},{16,20},{20,24},{24,28},{1,5},{5,9},{9,... | collective-permute-start | bytes 110600 | tf_op jit(solution)/shard_map/ppermute | solution.py:19
  100.6 11.0 %collective-permute-start.14 = (f32[6,6,12,2]{3,2,1,0:T(8,128)S(1)}, f32[6,6,12,2]{3,2,1,0:T(8,128)S(1)}, u32[]{:S(2)}, u32[]{:S(2)}) collective-permute-start(f32[6,6,12,2]{3,2,1,0:T(8,128)S(1)} %get-tuple-element.39), channel_id=1, source_target_pairs={{1,0},{2,1},{3,2},{5,4},{6,5},{7,6},{9,8},{10,9},{11,10},{13,12},{... | collective-permute-start | bytes 10376 | tf_op jit(solution)/shard_map/ppermute | solution.py:20
  104.0 10.7 %collective-permute-start.15 = (f32[6,6,12,2]{3,2,1,0:T(8,128)S(1)}, f32[6,6,12,2]{3,2,1,0:T(8,128)S(1)}, u32[]{:S(2)}, u32[]{:S(2)}) collective-permute-start(f32[6,6,12,2]{3,2,1,0:T(8,128)S(1)} %get-tuple-element.38), channel_id=1, source_target_pairs={{0,1},{1,2},{2,3},{4,5},{5,6},{6,7},{8,9},{9,10},{10,11},{12,13},{... | collective-permute-start | bytes 10376 | tf_op jit(solution)/shard_map/ppermute | solution.py:19
